TPU v7x, 256 devices: a whole 4x4x8 slice. The times are simulated.
256 devices in a mesh: seq: 32 (over z, x), head: 8 (over y, core).
Axes of the slice: x: 4, y: 4, z: 8, core: 2. Of those that a mesh axis runs over, the one named last changes fastest.
Arguments:
- queries: bfloat16 [32768, 2048], P('seq', 'head'), may hold values from -6 to 6
- keys: bfloat16 [32768, 2048], P('seq', 'head'), may hold values from -6 to 6
- values: bfloat16 [32768, 2048], P('seq', 'head'), may hold values from -6 to 6
- router_weight: bfloat16 [2048, 32], replicated, may hold values from -0.078125 to 0.078125
- gate_weight: bfloat16 [32, 2048, 512], P('seq'), may hold values from -0.125 to 0.125
- up_weight: bfloat16 [32, 2048, 512], P('seq'), may hold values from -0.125 to 0.125
- down_weight: bfloat16 [32, 2048, 512], P('seq'), may hold values from -0.5 to 0.5
- route_ids: int32 [32768, 8], P(('seq', 'head')), may hold values from 0 to 31, all different within a row; in each aligned block of 128 rows (0 to 127, 128 to 255, ...) at most 40 rows name the same one
Outputs:
- scored: bfloat16 [32768, 2048], P(('seq', 'head'))
Inputs may be any that keep to these rules, and one draw needn't show every extreme that they name: `route_ids`: in every aligned block of 128 rows (the rows of one device) each row names 8 different experts and no expert is named by more than 40 rows; some expert is named by exactly 40 rows of some block in every draw.
All inputs are finite; a program needn't handle non-finite values.
Results may differ from a plain program's by a relative error of at most 0.011.
Values may be sent and summed in bfloat16 or wider, within the bound.
A program may use at most 128 MiB of HBM per device.

v0:
```python
import jax
import jax.numpy as jnp
from jax import lax
from jax.sharding import PartitionSpec as P

HD = 128


epsilon = 1e-06


def entering(value, axis, combine, identity):
    devices, mine = (lax.axis_size(axis), lax.axis_index(axis))
    everything = lax.all_gather(value, axis)
    start = jnp.broadcast_to(jnp.asarray(identity, value.dtype), value.shape)

    def hop(k, before):
        reached = k < mine
        new = combine(before, everything[k])
        return jnp.where(reached, new, before)

    return lax.fori_loop(0, devices, hop, start)


def add_states(earlier, later):
    return earlier + later


def route_places(expert_ids, experts):
    blocks, block_rows, top_count = expert_ids.shape
    flat_ids = expert_ids.reshape(blocks, block_rows * top_count)
    onehot = (flat_ids[:, :, None] == jnp.arange(experts, dtype=jnp.int32)[None, None, :]).astype(
        jnp.int32
    )
    before = jnp.cumsum(onehot, axis=1) - onehot
    slot_rank = jnp.sum(before * onehot, axis=2)
    return (slot_rank * experts + flat_ids).reshape(blocks, block_rows, top_count)


def route_weights(logits, expert_ids):
    experts = logits.shape[-1]
    chosen = expert_ids[..., None] == jnp.arange(experts, dtype=jnp.int32)
    gate_score = jnp.sum(jnp.where(chosen, jax.nn.sigmoid(logits)[..., None, :], 0.0), axis=-1)
    return gate_score / jnp.sum(gate_score, axis=-1, keepdims=True)


def dispatch_matrix(places, slots_total):
    targets = jnp.arange(slots_total, dtype=jnp.int32)
    matches = jnp.any(places[:, None, :, :] == targets[None, :, None, None], axis=-1)
    return matches.astype(jnp.bfloat16)


def body(queries, keys, values, router_weight, gate_weight, up_weight, down_weight, route_ids):
    tok_dev, local_width = queries.shape
    heads_here = local_width // HD
    block_rows, top_count = route_ids.shape
    experts = router_weight.shape[1]
    capacity = min(block_rows, (block_rows * top_count * 5 + 4 * experts - 1) // (4 * experts))
    query_heads = queries.reshape(tok_dev, heads_here, HD)
    key_heads = keys.reshape(tok_dev, heads_here, HD)
    value_heads = values.reshape(tok_dev, heads_here, HD)
    local_state = jnp.einsum(
        "thd,the->hde", key_heads, value_heads, preferred_element_type=jnp.float32
    )
    carried = entering(local_state, "seq", add_states, jnp.zeros_like(local_state))
    scores = jnp.einsum("thd,shd->hts", query_heads, key_heads, preferred_element_type=jnp.float32)
    causal = jnp.arange(tok_dev)[:, None] >= jnp.arange(tok_dev)[None, :]
    scores = jnp.where(causal[None], scores, 0.0).astype(jnp.bfloat16)
    within = jnp.einsum("hts,she->the", scores, value_heads, preferred_element_type=jnp.float32)
    carried_part = jnp.einsum(
        "thd,hde->the", query_heads.astype(jnp.float32), carried, precision=lax.Precision.HIGHEST
    )
    attention = within + carried_part
    normed = attention * lax.rsqrt(
        jnp.mean(attention * attention, axis=-1, keepdims=True) + epsilon
    )
    normed = normed.astype(jnp.bfloat16).reshape(tok_dev, local_width)
    slots_total = capacity * experts
    token_rows = lax.all_to_all(normed, "head", split_axis=0, concat_axis=1, tiled=True)
    logits = jnp.dot(token_rows, router_weight, preferred_element_type=jnp.float32)
    weights = route_weights(logits, route_ids)
    block_places = route_places(route_ids[None], experts)
    selector = dispatch_matrix(block_places, slots_total)
    packed = jnp.einsum(
        "jcr,jrf->jcf", selector, token_rows[None], preferred_element_type=jnp.float32
    )
    packed = packed.astype(jnp.bfloat16).reshape(capacity, experts, token_rows.shape[1])
    arrived = lax.all_to_all(packed, "seq", split_axis=1, concat_axis=0, tiled=True)
    places = block_places[0]
    gate_part = jnp.einsum("med,edf->mef", arrived, gate_weight, preferred_element_type=jnp.float32)
    up_part = jnp.einsum("med,edf->mef", arrived, up_weight, preferred_element_type=jnp.float32)
    hidden = (jax.nn.silu(gate_part) * up_part).astype(jnp.bfloat16)
    produced = jnp.einsum(
        "mef,edf->med", hidden, down_weight, preferred_element_type=jnp.float32
    ).astype(jnp.bfloat16)
    returned = lax.all_to_all(produced, "seq", split_axis=0, concat_axis=1, tiled=True)
    model_width = returned.shape[2]
    flat_places = places.reshape(block_rows * top_count)
    picked = jnp.take(returned.reshape(slots_total, model_width), flat_places, axis=0).astype(
        jnp.float32
    )
    picked = picked.reshape(block_rows, top_count, model_width)
    return jnp.sum(weights[..., None] * picked, axis=1).astype(jnp.bfloat16)


def solution(mesh):
    in_specs = (
        P("seq", "head"),
        P("seq", "head"),
        P("seq", "head"),
        P(),
        P("seq", None, None),
        P("seq", None, None),
        P("seq", None, None),
        P(("seq", "head"), None),
    )
    out_specs = P(("seq", "head"), None)
    return jax.shard_map(body, mesh=mesh, in_specs=in_specs, out_specs=out_specs, check_vma=False)
```

profile of v0, /device:TPU:1, one launch (start us, length us, event | category | flops | bytes accessed | tf_op | source)
XLA Modules:
  0.0 488.6 jit_solution(2957168421815326060)
XLA Ops:
  8.0 2.2 fusion.21
  11.1 9.0 %reduce-window.6 = s32[1,32,8,128]{3,2,1,0:T(8,128)S(1)} reduce-window(s32[1,32,8,128]{3,2,1,0:T(8,128)S(1)} %bitcast.138, s32[]{:T(128)} %constant.55.clone.1), window={size=1x1x1x128 pad=0_0x0_0x0_0x127_0}, to_apply=%region_5.6 | reduce-window | flops 4161536 | bytes 262148 | tf_op jit(solution)/shard_map/reduce-window
  22.0 4.4 fusion.14
  26.3 66.9 %all-gather.3.cloned.1.call-done = f32[64,128,128]{2,1,0:T(8,128)} async-done(((f32[2,128,128]{2,1,0:T(8,128)}), f32[64,128,128]{2,1,0:T(8,128)}) %all-gather.3.cloned.1.call-update) | async-done | bytes 4194320 | tf_op jit(solution)/shard_map/all_gather | solution.py:14
  93.2 31.1 %while.14 = (s32[]{:T(128)}, f32[2,128,128]{2,1,0:T(8,128)S(1)}, s32[]{:T(128)}, f32[32,2,128,128]{3,2,1,0:T(8,128)}, s32[]{:T(128)}, /*index=5*/s32[]{:T(128)}) while((s32[]{:T(128)}, f32[2,128,128]{2,1,0:T(8,128)S(1)}, s32[]{:T(128)}, f32[32,2,128,128]{3,2,1,0:T(8,128)}, s32[]{:T(128)}, /*index=5*/s32[]{:T(128)}) %tuple.40), condition=%wide.region_1.2_spmd.clone, body=%wide.region_0.1_spmd.clone.sunk | while | flops 98308 | bytes 393317 | solution.py:22
  124.4 1.7 multiply_reduce_fusion.1
  127.2 7.6 %all-to-all-start = ((bf16[8,128,256]{1,2,0:T(8,128)(2,1)}), bf16[8,128,256]{1,2,0:T(8,128)(2,1)S(1)}, u32[]{:S(2)}, u32[]{:S(2)}) async-start(bf16[8,128,256]{1,2,0:T(8,128)(2,1)} %copy.95), calls=%async_computation | async-start | bytes 1048576 | tf_op jit(solution)/shard_map/all_to_all | solution.py:79
  135.0 4.6 fusion.1
  139.6 4.7 all-to-all-done
  144.3 1.5 convolution_convert_fusion.1
  145.8 2.9 copy.102
  148.7 121.4 %all_to_all.49 = bf16[40,32,2048]{2,0,1:T(8,128)(2,1)S(1)} all-to-all(bf16[40,32,2048]{2,0,1:T(8,128)(2,1)S(1)} %copy.102), channel_id=1, replica_groups=mesh['seq'=32,'head'=8] {'seq'}, dimensions={1} | all-to-all | bytes 10485760 | tf_op jit(solution)/shard_map/all_to_all | solution.py:88
  270.1 2.3 copy-done.2
  272.4 4.4 convolution_bitcast_fusion.1
  276.8 10.2 %fusion = bf16[1280,1,2048]{2,0,1:T(8,128)(2,1)} fusion(bf16[1,2048,512]{2,1,0:T(8,128)(2,1)S(1)} %copy-done, bf16[1280,2048]{1,0:T(8,128)(2,1)} %bitcast.131, f32[1280,1,512]{2,0,1:T(8,128)} %convolution_bitcast_fusion.1, bf16[1,2048,512]{2,1,0:T(8,128)(2,1)} %param.15), kind=kOutput, calls=%fused_computation.6 | convolution fusion | flops 5375262720 | bytes 17301504 | tf_op jit(solution)/shard_map/mef,edf->med/dot_general | solution.py:93
  287.6 8.4 %reduce.3 = bf16[1280,2048]{1,0:T(8,128)(2,1)} reduce(bf16[1280,1,2048]{2,0,1:T(8,128)(2,1)} %fusion, bf16[]{:T(256)} %broadcast.153), dimensions={1}, to_apply=%copy.103.reduce_sub_computation | reduce | bytes 10485762 | tf_op jit(solution)/shard_map/convert_element_type | solution.py:95
  296.0 13.1 %reshape.294 = bf16[32,2,40960]{2,1,0:T(2,128)(2,1)} reshape(bf16[1280,2048]{1,0:T(8,128)(2,1)} %reduce.3) | data formatting | bytes 10485760
  309.1 6.8 %all-to-all-start.2 = ((bf16[32,2,40960]{2,1,0:T(2,128)(2,1)}), bf16[32,2,40960]{2,1,0:T(2,128)(2,1)}, u32[]{:S(2)}, u32[]{:S(2)}) async-start(bf16[32,2,40960]{2,1,0:T(2,128)(2,1)} %reshape.294), calls=%async_computation.2 | async-start | bytes 10485760 | tf_op jit(solution)/shard_map/all_to_all | solution.py:96
  316.5 113.7 %all-to-all-done.2 = bf16[32,2,40960]{2,1,0:T(2,128)(2,1)} async-done(((bf16[32,2,40960]{2,1,0:T(2,128)(2,1)}), bf16[32,2,40960]{2,1,0:T(2,128)(2,1)}, u32[]{:S(2)}, u32[]{:S(2)}) %all-to-all-start.2) | async-done | bytes 5242912 | tf_op jit(solution)/shard_map/all_to_all | solution.py:96
  430.2 20.7 %reshape.295 = bf16[1280,1,2048]{2,1,0:T(2,128)(2,1)} reshape(bf16[32,2,40960]{2,1,0:T(2,128)(2,1)} %all-to-all-done.2) | data formatting | bytes 10485760
  450.8 7.3 %copy.107 = bf16[1280,1,2048]{2,0,1:T(8,128)(2,1)S(1)} copy(bf16[1280,1,2048]{2,1,0:T(2,128)(2,1)} %reshape.295) | data formatting | bytes 10485760
  458.1 5.2 %copy.104 = bf16[40,32,1,2048]{3,1,0,2:T(8,128)(2,1)} copy(bf16[40,32,1,2048]{3,0,1,2:T(8,128)(2,1)S(1)} %bitcast.129) | data formatting | bytes 10485760 | tf_op jit(solution)/shard_map/all_to_all | solution.py:96
  463.3 12.2 %gather_fusion = bf16[1024,2048]{1,0:T(8,128)(2,1)} fusion(bf16[1280,2048]{1,0:T(8,128)(2,1)} %bitcast.127, s32[1024]{0:T(1024)S(1)} %broadcast_clamp_fusion), kind=kCustom, calls=%fused_computation | custom fusion | bytes 8392704 | tf_op jit(solution)/shard_map/jit(_take)/gather | solution.py:99
  475.5 6.3 %multiply_reduce_fusion = bf16[128,2048]{1,0:T(8,128)(2,1)} fusion(bf16[1024,2048]{1,0:T(8,128)(2,1)} %gather_fusion, f32[128,8]{1,0:T(8,128)S(1)} %copy.96, pred[128,8]{1,0:T(8,128)(4,1)S(1)} %copy.101), kind=kLoop, calls=%fused_computation.2 | loop fusion | flops 8126464 | bytes 4723712 | tf_op jit(solution)/shard_map/reduce_sum | solution.py:103
  (80 shorter events, 36.9 us)
Async XLA Ops:
  6.5 270.3 %copy-start = (bf16[1,2048,512]{2,1,0:T(8,128)(2,1)S(1)}, bf16[1,2048,512]{2,1,0:T(8,128)(2,1)}, u32[]{:S(2)}) copy-start(bf16[1,2048,512]{2,1,0:T(8,128)(2,1)} %param.16) | copy-start | bytes 6291460
  6.5 86.7 %all-gather.3.cloned.1.call-start = ((), (), s32[]{:S(2)}) async-start(), calls=%async_computation.3 | async-start | bytes 4325376 | tf_op jit(solution)/shard_map/all_gather | solution.py:14
  7.9 3.1 copy-start.3
  124.3 10.6 %copy-start.5 = (s32[128,8]{0,1:T(8,128)S(1)}, s32[128,8]{0,1:T(8,128)}, u32[]{:S(2)}) copy-start(s32[128,8]{0,1:T(8,128)} %param.17) | copy-start | bytes 12292
  127.2 17.1 %all-to-all-start = ((bf16[8,128,256]{1,2,0:T(8,128)(2,1)}), bf16[8,128,256]{1,2,0:T(8,128)(2,1)S(1)}, u32[]{:S(2)}, u32[]{:S(2)}) async-start(bf16[8,128,256]{1,2,0:T(8,128)(2,1)} %copy.95), calls=%async_computation | async-start | bytes 1048576 | tf_op jit(solution)/shard_map/all_to_all | solution.py:79
  148.7 123.7 %copy-start.6 = (bf16[1,2048,512]{2,1,0:T(8,128)(2,1)S(1)}, bf16[1,2048,512]{2,1,0:T(8,128)(2,1)}, u32[]{:S(2)}) copy-start(bf16[1,2048,512]{2,1,0:T(8,128)(2,1)} %param.14) | copy-start | bytes 6291460
  270.1 2.3 copy-start.2
  309.1 7.0 %copy-start.4 = (bf16[2048,32]{0,1:T(8,128)(2,1)S(1)}, bf16[2048,32]{0,1:T(8,128)(2,1)}, u32[]{:S(2)}) copy-start(bf16[2048,32]{0,1:T(8,128)(2,1)} %param.13) | copy-start | bytes 393220
  309.1 121.1 %all-to-all-start.2 = ((bf16[32,2,40960]{2,1,0:T(2,128)(2,1)}), bf16[32,2,40960]{2,1,0:T(2,128)(2,1)}, u32[]{:S(2)}, u32[]{:S(2)}) async-start(bf16[32,2,40960]{2,1,0:T(2,128)(2,1)} %reshape.294), calls=%async_computation.2 | async-start | bytes 10485760 | tf_op jit(solution)/shard_map/all_to_all | solution.py:96
  463.3 18.5 %copy-start.1 = (bf16[1,2048,512]{2,1,0:T(8,128)(2,1)S(1)}, bf16[1,2048,512]{2,1,0:T(8,128)(2,1)}, u32[]{:S(2)}) copy-start(bf16[1,2048,512]{2,1,0:T(8,128)(2,1)} %param.16) | copy-start | bytes 6291460
Sparse Core Ops, SparseCore 0:
  10.3 82.9 all-gather.2
where the time goes:
time: 495 us; the launch traced here: 489 us
  waiting for transfers between devices  185 us (37%)
  blocking collectives  121 us (24%)
  local copies, waits for them, and re-layouts  68.3 us (14%)
  other arithmetic  60.3 us (12%)
  matrix products  24.7 us (5%)
  starting transfers between devices  14.4 us (3%)
  between operations  13.6 us (3%)
    all_to_all x1, blocking collectives, body(): lax.all_to_all(packed, 'seq', split_axis=1, concat_axis=0, tiled=True)  121 us
    all_to_all x1, waiting for transfers between devices, body(): lax.all_to_all(produced, 'seq', split_axis=0, concat_axis=1, tiled=True)  114 us
    all_gather x1, waiting for transfers between devices, entering(): everything = lax.all_gather(value, axis)  66.9 us
    unnamed x20, local copies, waits for them, and re-layouts  44.3 us
    select_n x32, other arithmetic, hop(): return jnp.where(reached, new, before)  30.4 us
    gather x1, local copies, waits for them, and re-layouts, body(): jnp.take(returned.reshape(slots_total, model_width), flat_places, axis=0)  12.2 us
    dot_general x1, matrix products, body(): jnp.einsum('mef,edf->med', hidden, down_weight, preferred_element_type=jn...  10.2 us
  transfers between devices with their start and end apart: 3, of which 3 were waited for; matrix products, arithmetic and copies ran while one was open for 4% of the time, Pallas kernels for 0%

commit v1 on v0

--- a/solution.py
+++ b/solution.py
@@ -29,11 +29,10 @@
 def route_places(expert_ids, experts):
     blocks, block_rows, top_count = expert_ids.shape
     flat_ids = expert_ids.reshape(blocks, block_rows * top_count)
-    onehot = (flat_ids[:, :, None] == jnp.arange(experts, dtype=jnp.int32)[None, None, :]).astype(
-        jnp.int32
-    )
-    before = jnp.cumsum(onehot, axis=1) - onehot
-    slot_rank = jnp.sum(before * onehot, axis=2)
+    pairs = block_rows * top_count
+    place = jnp.arange(pairs, dtype=jnp.int32)
+    same = (flat_ids[:, :, None] == flat_ids[:, None, :]) & (place[None, :, None] > place[None, None, :])
+    slot_rank = jnp.sum(same.astype(jnp.int32), axis=2)
     return (slot_rank * experts + flat_ids).reshape(blocks, block_rows, top_count)
 
 

time: 495 us -> 495 us (level)
  waiting for transfers between devices: 185 us -> 194 us
  other arithmetic: 60.3 us -> 51.7 us
    all_gather x1, waiting for transfers between devices: 66.9 us -> 76 us  [entering(): everything = lax.all_gather(value, axis)]
    another operation x2 -> x0, other arithmetic: 9.04 us -> none
    unnamed x20 -> x19, local copies, waits for them, and re-layouts: 44.3 us -> 44.3 us
  transfers between devices with their start and end apart: 3 -> 3, of which waited for: 3 -> 3; matrix products, arithmetic and copies ran while one was open for 4% -> 3% of each run, Pallas kernels for 0% -> 0%
where the time goes in v1:
time: 495 us; the launch traced here: 489 us
  waiting for transfers between devices  194 us (39%)
  blocking collectives  121 us (24%)
  local copies, waits for them, and re-layouts  67.9 us (14%)
  other arithmetic  51.7 us (10%)
  matrix products  24.7 us (5%)
  starting transfers between devices  14.4 us (3%)
  between operations  13.6 us (3%)
    all_to_all x1, blocking collectives, body(): lax.all_to_all(packed, 'seq', split_axis=1, concat_axis=0, tiled=True)  121 us
    all_to_all x1, waiting for transfers between devices, body(): lax.all_to_all(produced, 'seq', split_axis=0, concat_axis=1, tiled=True)  114 us
    all_gather x1, waiting for transfers between devices, entering(): everything = lax.all_gather(value, axis)  76 us
    unnamed x19, local copies, waits for them, and re-layouts  44.3 us
    select_n x32, other arithmetic, hop(): return jnp.where(reached, new, before)  30.4 us
    gather x1, local copies, waits for them, and re-layouts, body(): jnp.take(returned.reshape(slots_total, model_width), flat_places, axis=0)  12.2 us
    dot_general x1, matrix products, body(): jnp.einsum('mef,edf->med', hidden, down_weight, preferred_element_type=jn...  10.2 us
  transfers between devices with their start and end apart: 3, of which 3 were waited for; matrix products, arithmetic and copies ran while one was open for 3% of the time, Pallas kernels for 0%

profile of v1, /device:TPU:1, one launch (start us, length us, event | category | flops | bytes accessed | tf_op | source)
XLA Modules:
  0.0 488.6 jit_solution(7439303816782443574)
XLA Ops:
  6.5 1.4 copy.98
  8.0 2.2 fusion.22
  12.9 4.4 fusion.15
  17.2 76.0 %all-gather.3.cloned.1.call-done = f32[64,128,128]{2,1,0:T(8,128)} async-done(((f32[2,128,128]{2,1,0:T(8,128)}), f32[64,128,128]{2,1,0:T(8,128)}) %all-gather.3.cloned.1.call-update) | async-done | bytes 4194320 | tf_op jit(solution)/shard_map/all_gather | solution.py:14
  93.2 31.1 %while.14 = (s32[]{:T(128)}, f32[2,128,128]{2,1,0:T(8,128)S(1)}, s32[]{:T(128)}, f32[32,2,128,128]{3,2,1,0:T(8,128)}, s32[]{:T(128)}, /*index=5*/s32[]{:T(128)}) while((s32[]{:T(128)}, f32[2,128,128]{2,1,0:T(8,128)S(1)}, s32[]{:T(128)}, f32[32,2,128,128]{3,2,1,0:T(8,128)}, s32[]{:T(128)}, /*index=5*/s32[]{:T(128)}) %tuple.40), condition=%wide.region_1.2_spmd.clone, body=%wide.region_0.1_spmd.clone.sunk | while | flops 98308 | bytes 393317 | solution.py:22
  124.4 1.7 multiply_reduce_fusion.1
  127.2 7.6 %all-to-all-start = ((bf16[8,128,256]{1,2,0:T(8,128)(2,1)}), bf16[8,128,256]{1,2,0:T(8,128)(2,1)S(1)}, u32[]{:S(2)}, u32[]{:S(2)}) async-start(bf16[8,128,256]{1,2,0:T(8,128)(2,1)} %copy.87), calls=%async_computation | async-start | bytes 1048576 | tf_op jit(solution)/shard_map/all_to_all | solution.py:78
  135.0 4.6 fusion.1
  139.6 4.7 all-to-all-done
  144.3 1.5 convolution_convert_fusion.1
  145.8 2.9 copy.92
  148.7 121.4 %all_to_all.49 = bf16[40,32,2048]{2,0,1:T(8,128)(2,1)S(1)} all-to-all(bf16[40,32,2048]{2,0,1:T(8,128)(2,1)S(1)} %copy.92), channel_id=1, replica_groups=mesh['seq'=32,'head'=8] {'seq'}, dimensions={1} | all-to-all | bytes 10485760 | tf_op jit(solution)/shard_map/all_to_all | solution.py:87
  270.0 2.3 copy-done.2
  272.4 4.4 convolution_bitcast_fusion.1
  276.8 10.2 %fusion = bf16[1280,1,2048]{2,0,1:T(8,128)(2,1)} fusion(bf16[1,2048,512]{2,1,0:T(8,128)(2,1)S(1)} %copy-done, bf16[1280,2048]{1,0:T(8,128)(2,1)} %bitcast.118, f32[1280,1,512]{2,0,1:T(8,128)} %convolution_bitcast_fusion.1, bf16[1,2048,512]{2,1,0:T(8,128)(2,1)} %param.15), kind=kOutput, calls=%fused_computation.6 | convolution fusion | flops 5375262720 | bytes 17301504 | tf_op jit(solution)/shard_map/mef,edf->med/dot_general | solution.py:92
  287.6 8.4 %reduce.3 = bf16[1280,2048]{1,0:T(8,128)(2,1)} reduce(bf16[1280,1,2048]{2,0,1:T(8,128)(2,1)} %fusion, bf16[]{:T(256)} %broadcast.157), dimensions={1}, to_apply=%copy.93.reduce_sub_computation | reduce | bytes 10485762 | tf_op jit(solution)/shard_map/convert_element_type | solution.py:94
  296.0 13.1 %reshape.272 = bf16[32,2,40960]{2,1,0:T(2,128)(2,1)} reshape(bf16[1280,2048]{1,0:T(8,128)(2,1)} %reduce.3) | data formatting | bytes 10485760
  309.1 6.8 %all-to-all-start.2 = ((bf16[32,2,40960]{2,1,0:T(2,128)(2,1)}), bf16[32,2,40960]{2,1,0:T(2,128)(2,1)}, u32[]{:S(2)}, u32[]{:S(2)}) async-start(bf16[32,2,40960]{2,1,0:T(2,128)(2,1)} %reshape.272), calls=%async_computation.2 | async-start | bytes 10485760 | tf_op jit(solution)/shard_map/all_to_all | solution.py:95
  316.5 113.7 %all-to-all-done.2 = bf16[32,2,40960]{2,1,0:T(2,128)(2,1)} async-done(((bf16[32,2,40960]{2,1,0:T(2,128)(2,1)}), bf16[32,2,40960]{2,1,0:T(2,128)(2,1)}, u32[]{:S(2)}, u32[]{:S(2)}) %all-to-all-start.2) | async-done | bytes 5242912 | tf_op jit(solution)/shard_map/all_to_all | solution.py:95
  430.2 20.7 %reshape.273 = bf16[1280,1,2048]{2,1,0:T(2,128)(2,1)} reshape(bf16[32,2,40960]{2,1,0:T(2,128)(2,1)} %all-to-all-done.2) | data formatting | bytes 10485760
  450.8 7.3 %copy.97 = bf16[1280,1,2048]{2,0,1:T(8,128)(2,1)S(1)} copy(bf16[1280,1,2048]{2,1,0:T(2,128)(2,1)} %reshape.273) | data formatting | bytes 10485760
  458.1 5.2 %copy.94 = bf16[40,32,1,2048]{3,1,0,2:T(8,128)(2,1)} copy(bf16[40,32,1,2048]{3,0,1,2:T(8,128)(2,1)S(1)} %bitcast.116) | data formatting | bytes 10485760 | tf_op jit(solution)/shard_map/all_to_all | solution.py:95
  463.3 12.2 %gather_fusion = bf16[1024,2048]{1,0:T(8,128)(2,1)} fusion(bf16[1280,2048]{1,0:T(8,128)(2,1)} %bitcast.114, s32[1024]{0:T(1024)S(1)} %broadcast_clamp_fusion), kind=kCustom, calls=%fused_computation | custom fusion | bytes 8392704 | tf_op jit(solution)/shard_map/jit(_take)/gather | solution.py:98
  475.5 6.3 %multiply_reduce_fusion = bf16[128,2048]{1,0:T(8,128)(2,1)} fusion(bf16[1024,2048]{1,0:T(8,128)(2,1)} %gather_fusion, f32[128,8]{1,0:T(8,128)S(1)} %copy.88, pred[128,8]{1,0:T(8,128)(4,1)S(1)} %copy.91), kind=kLoop, calls=%fused_computation.2 | loop fusion | flops 8126464 | bytes 4723712 | tf_op jit(solution)/shard_map/reduce_sum | solution.py:102
  (69 shorter events, 35.5 us)
Async XLA Ops:
  6.5 270.3 %copy-start = (bf16[1,2048,512]{2,1,0:T(8,128)(2,1)S(1)}, bf16[1,2048,512]{2,1,0:T(8,128)(2,1)}, u32[]{:S(2)}) copy-start(bf16[1,2048,512]{2,1,0:T(8,128)(2,1)} %param.16) | copy-start | bytes 6291460
  6.5 86.7 %all-gather.3.cloned.1.call-start = ((), (), s32[]{:S(2)}) async-start(), calls=%async_computation.3 | async-start | bytes 4325376 | tf_op jit(solution)/shard_map/all_gather | solution.py:14
  7.9 2.2 copy-start.3
  124.3 10.6 %copy-start.5 = (s32[128,8]{0,1:T(8,128)S(1)}, s32[128,8]{0,1:T(8,128)}, u32[]{:S(2)}) copy-start(s32[128,8]{0,1:T(8,128)} %param.17) | copy-start | bytes 12292
  127.2 17.1 %all-to-all-start = ((bf16[8,128,256]{1,2,0:T(8,128)(2,1)}), bf16[8,128,256]{1,2,0:T(8,128)(2,1)S(1)}, u32[]{:S(2)}, u32[]{:S(2)}) async-start(bf16[8,128,256]{1,2,0:T(8,128)(2,1)} %copy.87), calls=%async_computation | async-start | bytes 1048576 | tf_op jit(solution)/shard_map/all_to_all | solution.py:78
  148.7 123.7 %copy-start.6 = (bf16[1,2048,512]{2,1,0:T(8,128)(2,1)S(1)}, bf16[1,2048,512]{2,1,0:T(8,128)(2,1)}, u32[]{:S(2)}) copy-start(bf16[1,2048,512]{2,1,0:T(8,128)(2,1)} %param.14) | copy-start | bytes 6291460
  270.0 2.3 copy-start.2
  309.1 7.1 %copy-start.4 = (bf16[2048,32]{0,1:T(8,128)(2,1)S(1)}, bf16[2048,32]{0,1:T(8,128)(2,1)}, u32[]{:S(2)}) copy-start(bf16[2048,32]{0,1:T(8,128)(2,1)} %param.13) | copy-start | bytes 393220
  309.1 121.1 %all-to-all-start.2 = ((bf16[32,2,40960]{2,1,0:T(2,128)(2,1)}), bf16[32,2,40960]{2,1,0:T(2,128)(2,1)}, u32[]{:S(2)}, u32[]{:S(2)}) async-start(bf16[32,2,40960]{2,1,0:T(2,128)(2,1)} %reshape.272), calls=%async_computation.2 | async-start | bytes 10485760 | tf_op jit(solution)/shard_map/all_to_all | solution.py:95
  463.3 18.5 %copy-start.1 = (bf16[1,2048,512]{2,1,0:T(8,128)(2,1)S(1)}, bf16[1,2048,512]{2,1,0:T(8,128)(2,1)}, u32[]{:S(2)}) copy-start(bf16[1,2048,512]{2,1,0:T(8,128)(2,1)} %param.16) | copy-start | bytes 6291460
Sparse Core Ops, SparseCore 0:
  10.3 82.9 all-gather.2

commit v2 on v1

v2 whole, which is shorter than its diff:
```python
import itertools

import jax
import jax.numpy as jnp
from jax import lax
from jax.experimental import pallas as pl
from jax.experimental.pallas import tpu as pltpu
from jax.sharding import PartitionSpec as P

HD = 128
NX, NZ, NY, NC = 4, 8, 4, 2
CAP = 40
epsilon = 1e-06
BF, F32 = jnp.bfloat16, jnp.float32
MESH = pl.DeviceIdType.MESH
NN, NT, TN = (((1,), (0,)), ((), ())), (((1,), (1,)), ((), ())), (((0,), (0,)), ((), ()))
FLOWS = 128


def dot(a, b, dims=NN):
    return lax.dot_general(a, b, dims, preferred_element_type=F32)


def kernel(q_hbm, k_hbm, v_hbm, rwt, g_hbm, u_hbm, d_hbm, idst, out_ref,
           qv, kv, vv, att, nrm, landed, tok, wv, xs, ys, part, rr, ll,
           st_out, st_in, tot, zs_out, zs_in, cz, car, meta_out, meta_in,
           ssem, rsem, lsem):
    seq, head = lax.axis_index("seq"), lax.axis_index("head")
    z, x = seq // NX, seq % NX
    y, c = head // NC, head % NC
    ids = itertools.count()
    sends = []

    def at_z(k):
        return lax.rem(z + k, NZ) * NX + x

    def at_x(k):
        return z * NX + lax.rem(x + k, NX)

    def at_h(k):
        return lax.rem(head + k, NY * NC)

    def at_y(k):
        return lax.rem(y + k, NY) * NC + c

    other_core = y * NC + (1 - c)

    def push(src, dst, to_seq, to_head):
        i = next(ids)
        cp = pltpu.make_async_remote_copy(
            src_ref=src, dst_ref=dst, send_sem=ssem.at[i], recv_sem=rsem.at[i],
            device_id=(to_seq, to_head), device_id_type=MESH)
        cp.start()
        sends.append(cp)
        return cp

    loads = [pltpu.make_async_copy(src, dst, lsem.at[i])
             for i, (src, dst) in enumerate(((k_hbm, kv), (v_hbm, vv), (q_hbm, qv)))]
    for cp in loads:
        cp.start()
    own = [pltpu.make_async_copy(src, wv.at[0, m], lsem.at[3 + m])
           for m, src in enumerate((g_hbm, u_hbm, d_hbm))]
    for cp in own:
        cp.start()

    barrier = pltpu.get_barrier_semaphore()
    partners = ([(at_x(k), head) for k in range(1, NX)] + [(at_z(k), head) for k in range(1, NZ)]
                + [(seq, at_h(k)) for k in range(1, NY * NC)])
    for to in partners:
        pl.semaphore_signal(barrier, inc=1, device_id=to, device_id_type=MESH)
    pl.semaphore_wait(barrier, len(partners))

    quarter = 2 * lax.rem(y, 2) + c
    across = 2 * (1 - lax.rem(y, 2)) + c
    hbm = (g_hbm, u_hbm, d_hbm)

    def x_send(m):
        src = hbm[m].at[quarter]
        return (push(src, wv.at[3, m, quarter], at_x(1), head), push(src, wv.at[1, m, quarter], at_x(3), head))

    def lo_hi(j, m, base):
        return wv.at[j, m, base, 0], wv.at[j, m, base, 1]

    def spread(j, m):
        lo, hi = lo_hi(j, m, quarter)
        full = wv.at[j, m, quarter]
        return (push(lo, lo, seq, at_y(1)), push(hi, hi, seq, at_y(3)), push(full, full, seq, other_core))

    def x_event(m, flows):
        right, left = flows
        right.wait_recv()
        lo, _ = lo_hi(3, m, quarter)
        f_right = push(lo, wv.at[2, m, quarter, 0], at_x(1), head)
        s3 = spread(3, m)
        left.wait_recv()
        _, hi = lo_hi(1, m, quarter)
        f_left = push(hi, wv.at[2, m, quarter, 1], at_x(3), head)
        s1 = spread(1, m)
        return (f_right, f_left), {3: s3, 1: s1}

    def f_event(m, flows):
        for cp in flows:
            cp.wait_recv()
        return spread(2, m)

    def y_event(j, m, flows):
        flows[0].wait_recv()
        flows[1].wait_recv()
        full = wv.at[j, m, across]
        return push(full, full, seq, other_core)

    xf = {0: x_send(0), 1: x_send(1)}
    fwd, spr, cor = {}, {}, {}

    def do_x(m):
        fwd[m], s = x_event(m, xf[m])
        spr[(3, m)], spr[(1, m)] = s[3], s[1]

    def do_y(j, m):
        cor[(j, m)] = y_event(j, m, spr[(j, m)])

    def do_f(m):
        spr[(2, m)] = f_event(m, fwd[m])

    def ready(j, m):
        if j == 0:
            own[m].wait()
        else:
            spr[(j, m)][2].wait_recv()
            cor[(j, m)].wait_recv()

    for cp in loads:
        cp.wait()
    for h in range(2):
        cols = slice(h * HD, (h + 1) * HD)
        s = dot(kv[:, cols], vv[:, cols], TN)
        tot[cols, :] = s
        st_out[cols, :] = s.astype(BF)
    st = [push(st_out, st_in.at[k - 1], at_x(k), head) for k in range(1, NX)]

    for h in range(2):
        cols = slice(h * HD, (h + 1) * HD)
        for i in range(4):
            qi = qv[i * 256:(i + 1) * 256, cols]
            acc = jnp.zeros((256, HD), F32)
            for j in range(i + 1):
                s = dot(qi, kv[j * 256:(j + 1) * 256, cols], NT)
                if i == j:
                    keep = (lax.broadcasted_iota(jnp.int32, (256, 256), 0)
                            >= lax.broadcasted_iota(jnp.int32, (256, 256), 1))
                    s = jnp.where(keep, s, 0.0)
                acc = acc + dot(s.astype(BF), vv[j * 256:(j + 1) * 256, cols])
            att[i * 256:(i + 1) * 256, cols] = acc

    before = jnp.zeros((2 * HD, HD), F32)
    total = tot[...]
    for k in range(1, NX):
        st[k - 1].wait_recv()
        came = st_in[k - 1].astype(F32)
        total = total + came
        before = before + came * (x >= k).astype(F32)
    tot[...] = total
    mine = pl.ds(pl.multiple_of(x * 64, 64), 64)
    zs_out[...] = tot[mine, :].astype(BF)
    zs = [push(zs_out, zs_in.at[k - 1], at_z(k), head) for k in range(1, NZ)]
    zq = jnp.zeros((64, HD), F32)
    for k in range(1, NZ):
        zs[k - 1].wait_recv()
        zq = zq + zs_in[k - 1].astype(F32) * (z >= k).astype(F32)
    cz[x] = zq.astype(BF)
    cs = [push(cz.at[x], cz.at[x], at_x(k), head) for k in range(1, NX)]
    do_x(0)
    xf[2] = x_send(2)
    for cp in cs:
        cp.wait_recv()
    carried = before + cz[...].astype(F32).reshape(2 * HD, HD)
    high = carried.astype(BF)
    car[0] = high
    car[1] = (carried - high.astype(F32)).astype(BF)

    a2a = []
    for k in range(NY * NC):
        owner = pl.ds(pl.multiple_of(at_h(k) * 128, 128), 128)
        for h in range(2):
            cols = slice(h * HD, (h + 1) * HD)
            qi = qv[owner, cols]
            a = att[owner, cols] + dot(qi, car[0, cols, :]) + dot(qi, car[1, cols, :])
            scale = lax.rsqrt(jnp.mean(a * a, axis=1, keepdims=True) + epsilon)
            nrm[k, :, cols] = (a * scale).astype(BF)
        if k > 0:
            a2a.append(push(nrm.at[k], landed.at[k - 1], seq, at_h(k)))
    do_x(1)
    for k in range(NY * NC):
        if k > 0:
            a2a[k - 1].wait_recv()
        hcols = pl.ds(pl.multiple_of(lax.rem(head + NY * NC - k, NY * NC) * 2 * HD, 2 * HD), 2 * HD)
        tok[0, 0, :, :, hcols] = (nrm[0] if k == 0 else landed[k - 1]).reshape(2, 64, 2 * HD)

    def half(ref, o, b):
        return ref.at[o // 2, o % 2, b]

    def ag(src, b, right):
        dst = (src + 7) % 8 if right else (src + 1) % 8
        return push(half(tok, src, b), half(tok, dst, b), at_z(1 if right else 7), head)

    ag_r, ag_l = {}, {}
    for b in range(2):
        ag_r[(7, b)] = ag(0, b, True)
        ag_l[(1, 1 - b)] = ag(0, 1 - b, False)

    lt = dot(rwt[...], tok[0, 0].reshape(128, rwt.shape[1]), NT)
    experts = lt.shape[0]
    number = lax.broadcasted_iota(jnp.int32, (experts, 128), 0)
    chosen = jnp.zeros((experts, 128), F32)
    for k in range(idst.shape[0]):
        chosen = chosen + jnp.where(number == idst[k:k + 1, :], 1.0, 0.0)
    score = jnp.where(chosen > 0.5, 1.0 / (1.0 + jnp.exp(-lt)), 0.0)
    weight = score / jnp.sum(score, axis=0, keepdims=True)
    earlier = (lax.broadcasted_iota(jnp.int32, (128, 128), 0)
               < lax.broadcasted_iota(jnp.int32, (128, 128), 1))
    rank = dot(chosen.astype(BF), jnp.where(earlier, 1.0, 0.0).astype(BF))
    rank = jnp.where(chosen > 0.5, rank, -1000.0)
    for p in range(NZ):
        meta_out[p, 0:NX, :] = rank[p * NX:(p + 1) * NX, :]
        meta_out[p, NX:2 * NX, :] = weight[p * NX:(p + 1) * NX, :]
    mt = [push(meta_out.at[lax.rem(z + k, NZ)], meta_in.at[8 - k], at_z(k), head) for k in range(1, NZ)]
    meta_in[0] = meta_out[z]

    def forward(o_r, o_l, b):
        ag_r[(o_r, b)].wait_recv()
        if not (o_r == 5 and b == 1):
            ag_r[(o_r - 1, b)] = ag(o_r, b, True)
        ag_l[(o_l, 1 - b)].wait_recv()
        if not (o_l == 3 and 1 - b == 0):
            ag_l[(o_l + 1, 1 - b)] = ag(o_l, 1 - b, False)

    slots = 2 * CAP

    def picks(pair, j):
        xj = lax.rem(x + j, NX)
        r0 = meta_in[2 * pair, pl.ds(xj, 1), :]
        r1 = meta_in[2 * pair + 1, pl.ds(xj, 1), :] + float(CAP)
        r = jnp.concatenate([r0, r1], axis=1)
        return lax.broadcasted_iota(jnp.int32, (slots, 256), 0).astype(F32) == r

    def picked_weight(pair, j):
        xj = lax.rem(x + j, NX)
        w = jnp.concatenate([meta_in[2 * pair, pl.ds(NX + xj, 1), :],
                             meta_in[2 * pair + 1, pl.ds(NX + xj, 1), :]], axis=1)
        return jnp.sum(jnp.where(picks(pair, j), w, 0.0), axis=1, keepdims=True)

    def all_picks(pair):
        return jnp.concatenate([jnp.where(picks(pair, j), 1.0, 0.0) for j in range(NX)], axis=0).astype(BF)

    def gather(lp, pair):
        p = all_picks(pair)
        for n in range(4):
            cols = slice(n * 512, (n + 1) * 512)
            got = dot(p, tok[pair, :, :, :, cols].reshape(256, 512)).astype(BF)
            for j in range(NX):
                xs[j, lp * slots:(lp + 1) * slots, cols] = got[j * slots:(j + 1) * slots, :]

    def whole(j, m):
        return wv[j, m].reshape(2048, 512)

    def expert(j, pairs):
        w = jnp.concatenate([picked_weight(pair, j) for pair in pairs], axis=0)
        rows_in = xs[j]
        gate = dot(rows_in, whole(j, 0))
        up = dot(rows_in, whole(j, 1))
        hidden = (gate / (1.0 + jnp.exp(-gate)) * up * w).astype(BF)
        for n in range(4):
            cols = slice(n * 512, (n + 1) * 512)
            made = dot(hidden, wv[j, 2, n].reshape(512, 512), NT).astype(BF)
            for lp in range(2):
                ys[lp, j * slots:(j + 1) * slots, cols] = made[lp * slots:(lp + 1) * slots, :]

    def combine(lp, pair):
        p = all_picks(pair)
        for n in range(4):
            cols = slice(n * 512, (n + 1) * 512)
            part[pair, :, :, :, cols] = dot(p, ys[lp, :, cols], TN).astype(BF).reshape(2, 2, 64, 512)

    near, far = (0, 3), (1, 2)
    forward(7, 1, 0)
    do_y(3, 0), do_y(1, 0)
    do_f(0)
    forward(7, 1, 1)
    for cp in mt:
        cp.wait_recv()
    gather(0, 0)
    do_x(2)
    do_y(3, 1), do_y(1, 1)
    forward(6, 2, 0)
    do_f(1)
    forward(6, 2, 1)
    gather(1, 3)
    do_y(2, 0)
    do_y(3, 2), do_y(1, 2)
    for m in range(3):
        ready(0, m)
    expert(0, near)
    forward(5, 3, 0)
    do_f(2)
    do_y(2, 1)
    for j in (3, 1):
        for m in range(3):
            ready(j, m)
        expert(j, near)
    forward(5, 3, 1)
    do_y(2, 2)
    for m in range(3):
        ready(2, m)
    expert(2, near)
    combine(0, 0)
    combine(1, 3)
    gather(0, 1)
    ag_r[(4, 0)].wait_recv()
    ag_l[(4, 1)].wait_recv()
    gather(1, 2)
    for j in range(NX):
        expert(j, far)

    def fold(buf, i, o, b):
        def step(r, carry):
            here = pl.ds(pl.multiple_of(r * 16, 16), 16)
            buf[i, here, :] = (buf[i, here, :].astype(F32) + part[o // 2, o % 2, b, here, :].astype(F32)).astype(BF)
            return carry
        lax.fori_loop(0, 4, step, 0)

    combine(1, 2)
    r_in, l_in = {}, {}
    r_in[0] = push(half(part, 4, 0), rr.at[0], at_z(1), head)
    l_in[0] = push(half(part, 4, 1), ll.at[0], at_z(7), head)
    l_in[2] = push(half(part, 5, 0), ll.at[2], at_z(7), head)
    combine(0, 1)
    r_in[2] = push(half(part, 3, 1), rr.at[2], at_z(1), head)
    for i, to, step in ((0, 1, 1), (1, 3, 2), (2, 4, 2), (3, 5, 3), (4, 6, 3)):
        b = {0: 0, 1: 0, 2: 1, 3: 0, 4: 1}[i]
        r_in[i].wait_recv()
        fold(rr, i, 4 - step, b)
        r_in[to] = push(rr.at[i], rr.at[to], at_z(1), head)
        l_in[i].wait_recv()
        fold(ll, i, 4 + step, 1 - b)
        l_in[to] = push(ll.at[i], ll.at[to], at_z(7), head)
    for b, (ri, li) in enumerate(((5, 6), (6, 5))):
        r_in[ri].wait_recv()
        l_in[li].wait_recv()

        def last(r, carry, b=b, ri=ri, li=li):
            here = pl.ds(pl.multiple_of(r * 16, 16), 16)
            there = pl.ds(pl.multiple_of(b * 64 + r * 16, 16), 16)
            out_ref[there, :] = (rr[ri, here, :].astype(F32) + ll[li, here, :].astype(F32)
                                 + part[0, 0, b, here, :].astype(F32)).astype(BF)
            return carry
        lax.fori_loop(0, 4, last, 0)
    for cp in sends:
        cp.wait_send()


def body(queries, keys, values, router_weight, gate_weight, up_weight, down_weight, route_ids):
    tok_dev, width = queries.shape
    block_rows, top_count = route_ids.shape
    dim, hidden = gate_weight.shape[1:]
    anywhere = pl.BlockSpec(memory_space=pl.ANY)
    vmem = pl.BlockSpec(memory_space=pltpu.VMEM)
    V = pltpu.VMEM
    return pl.pallas_call(
        kernel,
        out_shape=jax.ShapeDtypeStruct((block_rows, dim), BF),
        in_specs=[anywhere] * 3 + [vmem] + [anywhere] * 3 + [vmem],
        out_specs=vmem,
        scratch_shapes=[
            V((tok_dev, width), BF), V((tok_dev, width), BF), V((tok_dev, width), BF),
            V((tok_dev, width), F32), V((NY * NC, block_rows, width), BF), V((NY * NC - 1, block_rows, width), BF),
            V((NZ // 2, 2, 2, block_rows // 2, dim), BF),
            V((NX, 3, 4, 2, dim // 8, hidden), BF),
            V((NX, 4 * CAP, dim), BF), V((2, NX * 2 * CAP, dim), BF),
            V((NZ // 2, 2, 2, block_rows // 2, dim), BF),
            V((7, block_rows // 2, dim), BF), V((7, block_rows // 2, dim), BF),
            V((2 * HD, HD), BF), V((NX - 1, 2 * HD, HD), BF), V((2 * HD, HD), F32),
            V((64, HD), BF), V((NZ - 1, 64, HD), BF), V((NX, 64, HD), BF), V((2, 2 * HD, HD), BF),
            V((NZ, 2 * NX, block_rows), F32), V((NZ, 2 * NX, block_rows), F32),
            pltpu.SemaphoreType.DMA((FLOWS,)), pltpu.SemaphoreType.DMA((FLOWS,)),
            pltpu.SemaphoreType.DMA((8,)),
        ],
        compiler_params=pltpu.CompilerParams(
            collective_id=0, has_side_effects=True, vmem_limit_bytes=62 * 1024 * 1024),
        cost_estimate=pl.CostEstimate(flops=10 ** 10, bytes_accessed=10 ** 7, transcendentals=0),
    )(queries, keys, values, router_weight.T, *(w.reshape(4, 2, dim // 8, hidden) for w in (gate_weight, up_weight, down_weight)),
      route_ids.T)


def solution(mesh):
    in_specs = (
        P("seq", "head"),
        P("seq", "head"),
        P("seq", "head"),
        P(),
        P("seq", None, None),
        P("seq", None, None),
        P("seq", None, None),
        P(("seq", "head"), None),
    )
    out_specs = P(("seq", "head"), None)
    return jax.shard_map(body, mesh=mesh, in_specs=in_specs, out_specs=out_specs, check_vma=False)
```

time: 495 us -> 165 us (0.33); the launches traced: 489 us -> 165 us
  waiting for transfers between devices: 194 us -> 0 us
  Pallas kernels: 0 us -> 163 us
  blocking collectives: 121 us -> 0 us
  local copies, waits for them, and re-layouts: 67.9 us -> 1.88 us
  other arithmetic: 51.7 us -> 0 us
  matrix products: 24.7 us -> 0 us
  starting transfers between devices: 14.4 us -> 0 us
  between operations: 13.6 us -> 0.01 us
    pallas_call x0 -> x1, Pallas kernels: none -> 163 us  [body(): pl.pallas_call(kernel, out_shape=jax.ShapeDtypeStruct((block_rows, dim),...]
    all_to_all x1 -> x0, blocking collectives: 121 us -> none  [body(): lax.all_to_all(packed, 'seq', split_axis=1, concat_axis=0, tiled=True)]
    all_to_all x2 -> x0, waiting for transfers between devices: 118 us -> none  [the longest x1 114 us: body(): lax.all_to_all(produced, 'seq', split_axis=0, concat_axis=1, tiled=True)]
    all_gather x1 -> x0, waiting for transfers between devices: 76 us -> none  [entering(): everything = lax.all_gather(value, axis)]
    unnamed x19 -> x1, local copies, waits for them, and re-layouts: 44.3 us -> 1.88 us
    select_n x33 -> x0, other arithmetic: 30.4 us -> none  [the longest x32 30.4 us: hop(): return jnp.where(reached, new, before)]
    dot_general x7 -> x0, matrix products: 24.7 us -> none  [the longest x1 10.2 us: body(): jnp.einsum('mef,edf->med', hidden, down_weight, preferred_element_type=jn...]
    all_to_all x2 -> x0, starting transfers between devices: 14.4 us -> none  [the longest x1 7.59 us: body(): lax.all_to_all(normed, 'head', split_axis=0, concat_axis=1, tiled=True)]
  transfers between devices with their start and end apart: 3 -> 0, of which waited for: 3 -> 0; matrix products, arithmetic and copies ran while one was open for 3% -> 0% of each run, Pallas kernels for 0% -> 0%
where the time goes in v2:
time: 165 us
  Pallas kernels  163 us (99%)
  local copies, waits for them, and re-layouts  1.88 us (1%)
    pallas_call x1, Pallas kernels, body(): pl.pallas_call(kernel, out_shape=jax.ShapeDtypeStruct((block_rows, dim),...  163 us

profile of v2, /device:TPU:1, one launch (start us, length us, event | category | flops | bytes accessed | tf_op | source)
XLA Modules:
  0.0 164.6 jit_solution(2442029867468566537)
XLA Ops:
  0.0 162.7 %shard_map.82 = bf16[128,2048]{1,0:T(8,128)(2,1)} custom-call(bf16[1024,256]{1,0:T(8,128)(2,1)} %q_hbm.1, bf16[1024,256]{1,0:T(8,128)(2,1)} %k_hbm.1, bf16[1024,256]{1,0:T(8,128)(2,1)} %v_hbm.1, bf16[32,2048]{1,0:T(8,128)(2,1)} %bitcast.8, bf16[4,2,256,512]{3,2,1,0:T(8,128)(2,1)} %bitcast.5, bf16[4,2,256,512]{3,2,1,0:T(8,128)(2,1)} %bitcast.6, ...), custom_call_target="tpu_custom_call" | custom-call | flops 10000000000 | bytes 10000000 | tf_op jit(solution)/shard_map/pallas_call | solution.py:368
  162.7 1.9 %copy.10 = bf16[128,2048]{1,0:T(8,128)(2,1)} copy(bf16[128,2048]{1,0:T(8,128)(2,1)} %shard_map.82) | data formatting | bytes 1048576

commit v3 on v2

--- a/solution.py
+++ b/solution.py
@@ -14,7 +14,9 @@
 BF, F32 = jnp.bfloat16, jnp.float32
 MESH = pl.DeviceIdType.MESH
 NN, NT, TN = (((1,), (0,)), ((), ())), (((1,), (1,)), ((), ())), (((0,), (0,)), ((), ()))
-FLOWS = 128
+FLOWS = 160
+UNITS, COMMON_U = 32, 2
+OWN_U = (UNITS - 2 * COMMON_U) // 4
 
 
 def dot(a, b, dims=NN):
@@ -23,7 +25,7 @@
 
 def kernel(q_hbm, k_hbm, v_hbm, rwt, g_hbm, u_hbm, d_hbm, idst, out_ref,
            qv, kv, vv, att, nrm, landed, tok, wv, xs, ys, part, rr, ll,
-           st_out, st_in, tot, zs_out, zs_in, cz, car, meta_out, meta_in,
+           st_out, st_in, tot, zs_out, zs_in, cz_out, cz, car, meta_out, meta_in,
            ssem, rsem, lsem):
     seq, head = lax.axis_index("seq"), lax.axis_index("head")
     z, x = seq // NX, seq % NX
@@ -70,77 +72,93 @@
         pl.semaphore_signal(barrier, inc=1, device_id=to, device_id_type=MESH)
     pl.semaphore_wait(barrier, len(partners))
 
-    quarter = 2 * lax.rem(y, 2) + c
-    across = 2 * (1 - lax.rem(y, 2)) + c
+    quarter = (2 * lax.rem(y, 2) + c) * OWN_U
+    across = (2 * (1 - lax.rem(y, 2)) + c) * OWN_U
+    common = 4 * OWN_U + c * COMMON_U
     hbm = (g_hbm, u_hbm, d_hbm)
 
-    def x_send(m):
-        src = hbm[m].at[quarter]
-        return (push(src, wv.at[3, m, quarter], at_x(1), head), push(src, wv.at[1, m, quarter], at_x(3), head))
-
-    def lo_hi(j, m, base):
-        return wv.at[j, m, base, 0], wv.at[j, m, base, 1]
+    def part_of(j, m, start, count):
+        return wv.at[j, m, pl.ds(start, count)]
+
+    def same(j, m, start, count, to_seq, to_head):
+        piece = part_of(j, m, start, count)
+        return push(piece, piece, to_seq, to_head)
+
+    def x_send(m, start, count):
+        src = hbm[m].at[pl.ds(start, count)]
+        return (push(src, part_of(3, m, start, count), at_x(1), head),
+                push(src, part_of(1, m, start, count), at_x(3), head))
+
+    def low(j, m):
+        return OWN_U // 2 + (j + m) % 2 * (OWN_U % 2)
 
     def spread(j, m):
-        lo, hi = lo_hi(j, m, quarter)
-        full = wv.at[j, m, quarter]
-        return (push(lo, lo, seq, at_y(1)), push(hi, hi, seq, at_y(3)), push(full, full, seq, other_core))
-
-    def x_event(m, flows):
-        right, left = flows
+        n = low(j, m)
+        return (same(j, m, quarter, n, seq, at_y(1)), same(j, m, quarter + n, OWN_U - n, seq, at_y(3)),
+                same(j, m, quarter, OWN_U, seq, other_core))
+
+    xf, xc, fwd, fwc, spr, cor, com = {}, {}, {}, {}, {}, {}, {}
+
+    def do_x(m):
+        right, left = xf[m]
+        n = low(2, m)
         right.wait_recv()
-        lo, _ = lo_hi(3, m, quarter)
-        f_right = push(lo, wv.at[2, m, quarter, 0], at_x(1), head)
-        s3 = spread(3, m)
+        f_right = push(part_of(3, m, quarter, n), part_of(2, m, quarter, n), at_x(1), head)
+        spr[(3, m)] = spread(3, m)
         left.wait_recv()
-        _, hi = lo_hi(1, m, quarter)
-        f_left = push(hi, wv.at[2, m, quarter, 1], at_x(3), head)
-        s1 = spread(1, m)
-        return (f_right, f_left), {3: s3, 1: s1}
-
-    def f_event(m, flows):
-        for cp in flows:
+        f_left = push(part_of(1, m, quarter + n, OWN_U - n), part_of(2, m, quarter + n, OWN_U - n), at_x(3), head)
+        spr[(1, m)] = spread(1, m)
+        fwd[m] = (f_right, f_left)
+
+    def do_f(m):
+        for cp in fwd[m]:
             cp.wait_recv()
-        return spread(2, m)
-
-    def y_event(j, m, flows):
+        spr[(2, m)] = spread(2, m)
+
+    def do_y(j, m):
+        flows = spr[(j, m)]
         flows[0].wait_recv()
         flows[1].wait_recv()
-        full = wv.at[j, m, across]
-        return push(full, full, seq, other_core)
-
-    xf = {0: x_send(0), 1: x_send(1)}
-    fwd, spr, cor = {}, {}, {}
-
-    def do_x(m):
-        fwd[m], s = x_event(m, xf[m])
-        spr[(3, m)], spr[(1, m)] = s[3], s[1]
-
-    def do_y(j, m):
-        cor[(j, m)] = y_event(j, m, spr[(j, m)])
-
-    def do_f(m):
-        spr[(2, m)] = f_event(m, fwd[m])
-
-    def ready(j, m):
-        if j == 0:
-            own[m].wait()
-        else:
-            spr[(j, m)][2].wait_recv()
-            cor[(j, m)].wait_recv()
+        cor[(j, m)] = same(j, m, across, OWN_U, seq, other_core)
+
+    def do_c(m):
+        n = COMMON_U // 2
+        right, left = xc[m]
+        right.wait_recv()
+        f_right = push(part_of(3, m, common, n), part_of(2, m, common, n), at_x(1), head)
+        left.wait_recv()
+        f_left = push(part_of(1, m, common + n, COMMON_U - n), part_of(2, m, common + n, COMMON_U - n), at_x(3), head)
+        for j in (3, 1):
+            com[(j, m)] = same(j, m, common, COMMON_U, seq, other_core)
+        fwc[m] = (f_right, f_left)
+
+    def do_fc(m):
+        for cp in fwc[m]:
+            cp.wait_recv()
+        com[(2, m)] = same(2, m, common, COMMON_U, seq, other_core)
+
+    def ready(j):
+        for m in range(3):
+            if j == 0:
+                own[m].wait()
+            else:
+                spr[(j, m)][2].wait_recv()
+                cor[(j, m)].wait_recv()
+                com[(j, m)].wait_recv()
 
     for cp in loads:
         cp.wait()
     for h in range(2):
         cols = slice(h * HD, (h + 1) * HD)
         s = dot(kv[:, cols], vv[:, cols], TN)
-        tot[cols, :] = s
-        st_out[cols, :] = s.astype(BF)
-    st = [push(st_out, st_in.at[k - 1], at_x(k), head) for k in range(1, NX)]
-
-    for h in range(2):
+        for i in range(2):
+            tot[2 * h + i] = s[i * 64:(i + 1) * 64, :]
+            st_out[2 * h + i] = s[i * 64:(i + 1) * 64, :].astype(BF)
+    st = [push(st_out.at[lax.rem(x + k, NX)], st_in.at[k - 1], at_x(k), head) for k in range(1, NX)]
+
+    def intra(h, tiles):
         cols = slice(h * HD, (h + 1) * HD)
-        for i in range(4):
+        for i in tiles:
             qi = qv[i * 256:(i + 1) * 256, cols]
             acc = jnp.zeros((256, HD), F32)
             for j in range(i + 1):
@@ -152,28 +170,36 @@
                 acc = acc + dot(s.astype(BF), vv[j * 256:(j + 1) * 256, cols])
             att[i * 256:(i + 1) * 256, cols] = acc
 
-    before = jnp.zeros((2 * HD, HD), F32)
-    total = tot[...]
+    intra(0, (0, 1, 2))
+    total = tot[x]
     for k in range(1, NX):
         st[k - 1].wait_recv()
-        came = st_in[k - 1].astype(F32)
-        total = total + came
-        before = before + came * (x >= k).astype(F32)
-    tot[...] = total
-    mine = pl.ds(pl.multiple_of(x * 64, 64), 64)
-    zs_out[...] = tot[mine, :].astype(BF)
+        total = total + st_in[k - 1].astype(F32)
+    zs_out[...] = total.astype(BF)
     zs = [push(zs_out, zs_in.at[k - 1], at_z(k), head) for k in range(1, NZ)]
+    intra(0, (3,))
+    intra(1, (0, 1, 2, 3))
     zq = jnp.zeros((64, HD), F32)
     for k in range(1, NZ):
         zs[k - 1].wait_recv()
         zq = zq + zs_in[k - 1].astype(F32) * (z >= k).astype(F32)
-    cz[x] = zq.astype(BF)
-    cs = [push(cz.at[x], cz.at[x], at_x(k), head) for k in range(1, NX)]
-    do_x(0)
-    xf[2] = x_send(2)
+    own_state = tot[x]
+    for k in range(NX):
+        to = lax.rem(x + k, NX)
+        entering = zq + own_state * (to > x).astype(F32)
+        for i in range(1, NX):
+            came_from = lax.rem(x + NX - i, NX)
+            entering = entering + st_in[i - 1].astype(F32) * (to > came_from).astype(F32)
+        if k == 0:
+            cz[x] = entering
+        else:
+            cz_out[k - 1] = entering
+    cs = [push(cz_out.at[k - 1], cz.at[x], at_x(k), head) for k in range(1, NX)]
     for cp in cs:
         cp.wait_recv()
-    carried = before + cz[...].astype(F32).reshape(2 * HD, HD)
+    for m in range(3):
+        xf[m] = x_send(m, quarter, OWN_U)
+    carried = cz[...].reshape(2 * HD, HD)
     high = carried.astype(BF)
     car[0] = high
     car[1] = (carried - high.astype(F32)).astype(BF)
@@ -189,7 +215,6 @@
             nrm[k, :, cols] = (a * scale).astype(BF)
         if k > 0:
             a2a.append(push(nrm.at[k], landed.at[k - 1], seq, at_h(k)))
-    do_x(1)
     for k in range(NY * NC):
         if k > 0:
             a2a[k - 1].wait_recv()
@@ -252,74 +277,77 @@
     def all_picks(pair):
         return jnp.concatenate([jnp.where(picks(pair, j), 1.0, 0.0) for j in range(NX)], axis=0).astype(BF)
 
-    def gather(lp, pair):
+    def gather(batch, lp, pair):
         p = all_picks(pair)
         for n in range(4):
             cols = slice(n * 512, (n + 1) * 512)
             got = dot(p, tok[pair, :, :, :, cols].reshape(256, 512)).astype(BF)
             for j in range(NX):
-                xs[j, lp * slots:(lp + 1) * slots, cols] = got[j * slots:(j + 1) * slots, :]
+                xs[batch, j, lp * slots:(lp + 1) * slots, cols] = got[j * slots:(j + 1) * slots, :]
 
     def whole(j, m):
         return wv[j, m].reshape(2048, 512)
 
-    def expert(j, pairs):
+    def expert(j, batch, pairs):
         w = jnp.concatenate([picked_weight(pair, j) for pair in pairs], axis=0)
-        rows_in = xs[j]
+        rows_in = xs[batch, j]
         gate = dot(rows_in, whole(j, 0))
         up = dot(rows_in, whole(j, 1))
         hidden = (gate / (1.0 + jnp.exp(-gate)) * up * w).astype(BF)
         for n in range(4):
             cols = slice(n * 512, (n + 1) * 512)
-            made = dot(hidden, wv[j, 2, n].reshape(512, 512), NT).astype(BF)
-            for lp in range(2):
-                ys[lp, j * slots:(j + 1) * slots, cols] = made[lp * slots:(lp + 1) * slots, :]
-
-    def combine(lp, pair):
+            made = dot(hidden, wv[j, 2, n * 8:(n + 1) * 8].reshape(512, 512), NT).astype(BF)
+            for lp, pair in enumerate(pairs):
+                ys[pair, j * slots:(j + 1) * slots, cols] = made[lp * slots:(lp + 1) * slots, :]
+
+    def combine(pair):
         p = all_picks(pair)
         for n in range(4):
             cols = slice(n * 512, (n + 1) * 512)
-            part[pair, :, :, :, cols] = dot(p, ys[lp, :, cols], TN).astype(BF).reshape(2, 2, 64, 512)
+            part[pair, :, :, :, cols] = dot(p, ys[pair, :, cols], TN).astype(BF).reshape(2, 2, 64, 512)
 
     near, far = (0, 3), (1, 2)
+    do_x(0)
     forward(7, 1, 0)
-    do_y(3, 0), do_y(1, 0)
-    do_f(0)
     forward(7, 1, 1)
     for cp in mt:
         cp.wait_recv()
-    gather(0, 0)
+    gather(0, 0, 0)
+    do_x(1)
+    do_y(3, 0), do_y(1, 0)
+    forward(6, 2, 0)
+    forward(6, 2, 1)
+    gather(0, 1, 3)
+    ready(0)
     do_x(2)
+    for m in range(3):
+        xc[m] = x_send(m, common, COMMON_U)
+    forward(5, 3, 0)
     do_y(3, 1), do_y(1, 1)
-    forward(6, 2, 0)
+    expert(0, 0, near)
+    do_f(0)
+    forward(5, 3, 1)
+    gather(1, 0, 1)
     do_f(1)
-    forward(6, 2, 1)
-    gather(1, 3)
+    do_y(3, 2), do_y(1, 2)
+    do_f(2)
+    ag_r[(4, 0)].wait_recv()
+    ag_l[(4, 1)].wait_recv()
+    gather(1, 1, 2)
+    do_c(0), do_c(1), do_c(2)
     do_y(2, 0)
-    do_y(3, 2), do_y(1, 2)
-    for m in range(3):
-        ready(0, m)
-    expert(0, near)
-    forward(5, 3, 0)
-    do_f(2)
+    expert(0, 1, far)
     do_y(2, 1)
     for j in (3, 1):
-        for m in range(3):
-            ready(j, m)
-        expert(j, near)
-    forward(5, 3, 1)
+        ready(j)
+        expert(j, 1, far)
+        if j == 3:
+            do_fc(0), do_fc(1)
     do_y(2, 2)
-    for m in range(3):
-        ready(2, m)
-    expert(2, near)
-    combine(0, 0)
-    combine(1, 3)
-    gather(0, 1)
-    ag_r[(4, 0)].wait_recv()
-    ag_l[(4, 1)].wait_recv()
-    gather(1, 2)
-    for j in range(NX):
-        expert(j, far)
+    do_fc(2)
+    expert(3, 0, near)
+    ready(2)
+    expert(2, 1, far)
 
     def fold(buf, i, o, b):
         def step(r, carry):
@@ -328,13 +356,17 @@
             return carry
         lax.fori_loop(0, 4, step, 0)
 
-    combine(1, 2)
+    combine(2)
     r_in, l_in = {}, {}
     r_in[0] = push(half(part, 4, 0), rr.at[0], at_z(1), head)
     l_in[0] = push(half(part, 4, 1), ll.at[0], at_z(7), head)
     l_in[2] = push(half(part, 5, 0), ll.at[2], at_z(7), head)
-    combine(0, 1)
+    combine(1)
     r_in[2] = push(half(part, 3, 1), rr.at[2], at_z(1), head)
+    for j in (1, 2):
+        expert(j, 0, near)
+    combine(3)
+    combine(0)
     for i, to, step in ((0, 1, 1), (1, 3, 2), (2, 4, 2), (3, 5, 3), (4, 6, 3)):
         b = {0: 0, 1: 0, 2: 1, 3: 0, 4: 1}[i]
         r_in[i].wait_recv()
@@ -374,12 +406,12 @@
             V((tok_dev, width), BF), V((tok_dev, width), BF), V((tok_dev, width), BF),
             V((tok_dev, width), F32), V((NY * NC, block_rows, width), BF), V((NY * NC - 1, block_rows, width), BF),
             V((NZ // 2, 2, 2, block_rows // 2, dim), BF),
-            V((NX, 3, 4, 2, dim // 8, hidden), BF),
-            V((NX, 4 * CAP, dim), BF), V((2, NX * 2 * CAP, dim), BF),
+            V((NX, 3, UNITS, dim // UNITS, hidden), BF),
+            V((2, NX, 4 * CAP, dim), BF), V((NZ // 2, NX * 2 * CAP, dim), BF),
             V((NZ // 2, 2, 2, block_rows // 2, dim), BF),
             V((7, block_rows // 2, dim), BF), V((7, block_rows // 2, dim), BF),
-            V((2 * HD, HD), BF), V((NX - 1, 2 * HD, HD), BF), V((2 * HD, HD), F32),
-            V((64, HD), BF), V((NZ - 1, 64, HD), BF), V((NX, 64, HD), BF), V((2, 2 * HD, HD), BF),
+            V((NX, 64, HD), BF), V((NX - 1, 64, HD), BF), V((NX, 64, HD), F32),
+            V((64, HD), BF), V((NZ - 1, 64, HD), BF), V((NX - 1, 64, HD), F32), V((NX, 64, HD), F32), V((2, 2 * HD, HD), BF),
             V((NZ, 2 * NX, block_rows), F32), V((NZ, 2 * NX, block_rows), F32),
             pltpu.SemaphoreType.DMA((FLOWS,)), pltpu.SemaphoreType.DMA((FLOWS,)),
             pltpu.SemaphoreType.DMA((8,)),
@@ -387,7 +419,7 @@
         compiler_params=pltpu.CompilerParams(
             collective_id=0, has_side_effects=True, vmem_limit_bytes=62 * 1024 * 1024),
         cost_estimate=pl.CostEstimate(flops=10 ** 10, bytes_accessed=10 ** 7, transcendentals=0),
-    )(queries, keys, values, router_weight.T, *(w.reshape(4, 2, dim // 8, hidden) for w in (gate_weight, up_weight, down_weight)),
+    )(queries, keys, values, router_weight.T, *(w.reshape(UNITS, dim // UNITS, hidden) for w in (gate_weight, up_weight, down_weight)),
       route_ids.T)
 
 

time: 165 us -> 138 us (0.84)
  Pallas kernels: 163 us -> 136 us
    pallas_call x1, Pallas kernels: 163 us -> 136 us  [body(): pl.pallas_call(kernel, out_shape=jax.ShapeDtypeStruct((block_rows, dim),...]
where the time goes in v3:
time: 138 us
  Pallas kernels  136 us (99%)
  local copies, waits for them, and re-layouts  1.88 us (1%)
    pallas_call x1, Pallas kernels, body(): pl.pallas_call(kernel, out_shape=jax.ShapeDtypeStruct((block_rows, dim),...  136 us

profile of v3, /device:TPU:1, one launch (start us, length us, event | category | flops | bytes accessed | tf_op | source)
XLA Modules:
  0.0 138.2 jit_solution(18082587445962782607)
XLA Ops:
  0.0 136.3 %shard_map.82 = bf16[128,2048]{1,0:T(8,128)(2,1)} custom-call(bf16[1024,256]{1,0:T(8,128)(2,1)} %q_hbm.1, bf16[1024,256]{1,0:T(8,128)(2,1)} %k_hbm.1, bf16[1024,256]{1,0:T(8,128)(2,1)} %v_hbm.1, bf16[32,2048]{1,0:T(8,128)(2,1)} %bitcast.8, bf16[32,64,512]{2,1,0:T(8,128)(2,1)} %bitcast.5, bf16[32,64,512]{2,1,0:T(8,128)(2,1)} %bitcast.6, ...), custom_call_target="tpu_custom_call" | custom-call | flops 10000000000 | bytes 10000000 | tf_op jit(solution)/shard_map/pallas_call | solution.py:400
  136.4 1.9 %copy.10 = bf16[128,2048]{1,0:T(8,128)(2,1)} copy(bf16[128,2048]{1,0:T(8,128)(2,1)} %shard_map.82) | data formatting | bytes 1048576

commit v4 on v3

--- a/solution.py
+++ b/solution.py
@@ -17,6 +17,8 @@
 FLOWS = 160
 UNITS, COMMON_U = 32, 2
 OWN_U = (UNITS - 2 * COMMON_U) // 4
+ORDER = (0, 4, 1, 7, 2, 6, 3, 5)
+PIECES = ((0, 0, 3), (0, 3, OWN_U - 3), (1, 0, OWN_U), (2, 0, OWN_U))
 
 
 def dot(a, b, dims=NN):
@@ -89,37 +91,45 @@
         return (push(src, part_of(3, m, start, count), at_x(1), head),
                 push(src, part_of(1, m, start, count), at_x(3), head))
 
-    def low(j, m):
-        return OWN_U // 2 + (j + m) % 2 * (OWN_U % 2)
-
-    def spread(j, m):
-        n = low(j, m)
-        return (same(j, m, quarter, n, seq, at_y(1)), same(j, m, quarter + n, OWN_U - n, seq, at_y(3)),
-                same(j, m, quarter, OWN_U, seq, other_core))
+    def low(j, i):
+        count = PIECES[i][2]
+        return count // 2 + (j + i) % 2 * (count % 2)
+
+    def spread(j, i):
+        m, first, count = PIECES[i]
+        n, start = low(j, i), quarter + first
+        return (same(j, m, start, n, seq, at_y(1)), same(j, m, start + n, count - n, seq, at_y(3)),
+                same(j, m, start, count, seq, other_core))
 
     xf, xc, fwd, fwc, spr, cor, com = {}, {}, {}, {}, {}, {}, {}
 
-    def do_x(m):
-        right, left = xf[m]
-        n = low(2, m)
+    def send(i):
+        m, first, count = PIECES[i]
+        xf[i] = x_send(m, quarter + first, count)
+
+    def do_x(i):
+        m, first, count = PIECES[i]
+        right, left = xf[i]
+        n, start = low(2, i), quarter + first
         right.wait_recv()
-        f_right = push(part_of(3, m, quarter, n), part_of(2, m, quarter, n), at_x(1), head)
-        spr[(3, m)] = spread(3, m)
+        f_right = push(part_of(3, m, start, n), part_of(2, m, start, n), at_x(1), head)
+        spr[(3, i)] = spread(3, i)
         left.wait_recv()
-        f_left = push(part_of(1, m, quarter + n, OWN_U - n), part_of(2, m, quarter + n, OWN_U - n), at_x(3), head)
-        spr[(1, m)] = spread(1, m)
-        fwd[m] = (f_right, f_left)
-
-    def do_f(m):
-        for cp in fwd[m]:
+        f_left = push(part_of(1, m, start + n, count - n), part_of(2, m, start + n, count - n), at_x(3), head)
+        spr[(1, i)] = spread(1, i)
+        fwd[i] = (f_right, f_left)
+
+    def do_f(i):
+        for cp in fwd[i]:
             cp.wait_recv()
-        spr[(2, m)] = spread(2, m)
-
-    def do_y(j, m):
-        flows = spr[(j, m)]
+        spr[(2, i)] = spread(2, i)
+
+    def do_y(j, i):
+        m, first, count = PIECES[i]
+        flows = spr[(j, i)]
         flows[0].wait_recv()
         flows[1].wait_recv()
-        cor[(j, m)] = same(j, m, across, OWN_U, seq, other_core)
+        cor[(j, i)] = same(j, m, across + first, count, seq, other_core)
 
     def do_c(m):
         n = COMMON_U // 2
@@ -142,10 +152,13 @@
             if j == 0:
                 own[m].wait()
             else:
-                spr[(j, m)][2].wait_recv()
-                cor[(j, m)].wait_recv()
                 com[(j, m)].wait_recv()
-
+        if j > 0:
+            for i in range(len(PIECES)):
+                spr[(j, i)][2].wait_recv()
+                cor[(j, i)].wait_recv()
+
+    send(0)
     for cp in loads:
         cp.wait()
     for h in range(2):
@@ -177,8 +190,10 @@
         total = total + st_in[k - 1].astype(F32)
     zs_out[...] = total.astype(BF)
     zs = [push(zs_out, zs_in.at[k - 1], at_z(k), head) for k in range(1, NZ)]
+    send(1)
     intra(0, (3,))
     intra(1, (0, 1, 2, 3))
+    do_x(0)
     zq = jnp.zeros((64, HD), F32)
     for k in range(1, NZ):
         zs[k - 1].wait_recv()
@@ -195,34 +210,39 @@
         else:
             cz_out[k - 1] = entering
     cs = [push(cz_out.at[k - 1], cz.at[x], at_x(k), head) for k in range(1, NX)]
+    do_x(1)
     for cp in cs:
         cp.wait_recv()
-    for m in range(3):
-        xf[m] = x_send(m, quarter, OWN_U)
+    send(2)
+    send(3)
     carried = cz[...].reshape(2 * HD, HD)
     high = carried.astype(BF)
     car[0] = high
     car[1] = (carried - high.astype(F32)).astype(BF)
 
-    a2a = []
-    for k in range(NY * NC):
-        owner = pl.ds(pl.multiple_of(at_h(k) * 128, 128), 128)
-        for h in range(2):
-            cols = slice(h * HD, (h + 1) * HD)
-            qi = qv[owner, cols]
-            a = att[owner, cols] + dot(qi, car[0, cols, :]) + dot(qi, car[1, cols, :])
-            scale = lax.rsqrt(jnp.mean(a * a, axis=1, keepdims=True) + epsilon)
-            nrm[k, :, cols] = (a * scale).astype(BF)
-        if k > 0:
-            a2a.append(push(nrm.at[k], landed.at[k - 1], seq, at_h(k)))
-    for k in range(NY * NC):
-        if k > 0:
-            a2a[k - 1].wait_recv()
-        hcols = pl.ds(pl.multiple_of(lax.rem(head + NY * NC - k, NY * NC) * 2 * HD, 2 * HD), 2 * HD)
-        tok[0, 0, :, :, hcols] = (nrm[0] if k == 0 else landed[k - 1]).reshape(2, 64, 2 * HD)
+    a2a = {}
+    for b in range(2):
+        for k in range(NY * NC):
+            owned = pl.ds(pl.multiple_of(at_h(k) * 128 + b * 64, 64), 64)
+            for h in range(2):
+                cols = slice(h * HD, (h + 1) * HD)
+                qi = qv[owned, cols]
+                a = att[owned, cols] + dot(qi, car[0, cols, :]) + dot(qi, car[1, cols, :])
+                scale = lax.rsqrt(jnp.mean(a * a, axis=1, keepdims=True) + epsilon)
+                nrm[b, k, :, cols] = (a * scale).astype(BF)
+            if k > 0:
+                a2a[(b, k)] = push(nrm.at[b, k], landed.at[b, k - 1], seq, at_h(k))
+
+    def assemble(b):
+        for k in range(NY * NC):
+            if k > 0:
+                a2a[(b, k)].wait_recv()
+            hcols = pl.ds(pl.multiple_of(lax.rem(head + NY * NC - k, NY * NC) * 2 * HD, 2 * HD), 2 * HD)
+            tok[0, 0, b, :, hcols] = nrm[b, 0] if k == 0 else landed[b, k - 1]
 
     def half(ref, o, b):
-        return ref.at[o // 2, o % 2, b]
+        at = ORDER.index(o)
+        return ref.at[at // 2, at % 2, b]
 
     def ag(src, b, right):
         dst = (src + 7) % 8 if right else (src + 1) % 8
@@ -230,9 +250,11 @@
 
     ag_r, ag_l = {}, {}
     for b in range(2):
+        assemble(b)
         ag_r[(7, b)] = ag(0, b, True)
-        ag_l[(1, 1 - b)] = ag(0, 1 - b, False)
-
+        ag_l[(1, b)] = ag(0, b, False)
+
+    do_f(0), do_f(1)
     lt = dot(rwt[...], tok[0, 0].reshape(128, rwt.shape[1]), NT)
     experts = lt.shape[0]
     number = lax.broadcasted_iota(jnp.int32, (experts, 128), 0)
@@ -255,23 +277,23 @@
         ag_r[(o_r, b)].wait_recv()
         if not (o_r == 5 and b == 1):
             ag_r[(o_r - 1, b)] = ag(o_r, b, True)
-        ag_l[(o_l, 1 - b)].wait_recv()
-        if not (o_l == 3 and 1 - b == 0):
-            ag_l[(o_l + 1, 1 - b)] = ag(o_l, 1 - b, False)
+        ag_l[(o_l, b)].wait_recv()
+        if not (o_l == 3 and b == 0):
+            ag_l[(o_l + 1, b)] = ag(o_l, b, False)
 
     slots = 2 * CAP
 
     def picks(pair, j):
         xj = lax.rem(x + j, NX)
-        r0 = meta_in[2 * pair, pl.ds(xj, 1), :]
-        r1 = meta_in[2 * pair + 1, pl.ds(xj, 1), :] + float(CAP)
+        r0 = meta_in[ORDER[2 * pair], pl.ds(xj, 1), :]
+        r1 = meta_in[ORDER[2 * pair + 1], pl.ds(xj, 1), :] + float(CAP)
         r = jnp.concatenate([r0, r1], axis=1)
         return lax.broadcasted_iota(jnp.int32, (slots, 256), 0).astype(F32) == r
 
     def picked_weight(pair, j):
         xj = lax.rem(x + j, NX)
-        w = jnp.concatenate([meta_in[2 * pair, pl.ds(NX + xj, 1), :],
-                             meta_in[2 * pair + 1, pl.ds(NX + xj, 1), :]], axis=1)
+        w = jnp.concatenate([meta_in[ORDER[2 * pair], pl.ds(NX + xj, 1), :],
+                             meta_in[ORDER[2 * pair + 1], pl.ds(NX + xj, 1), :]], axis=1)
         return jnp.sum(jnp.where(picks(pair, j), w, 0.0), axis=1, keepdims=True)
 
     def all_picks(pair):
@@ -288,9 +310,9 @@
     def whole(j, m):
         return wv[j, m].reshape(2048, 512)
 
-    def expert(j, batch, pairs):
+    def expert(j, batch, first, pairs):
         w = jnp.concatenate([picked_weight(pair, j) for pair in pairs], axis=0)
-        rows_in = xs[batch, j]
+        rows_in = xs[batch, j, first * slots:(first + len(pairs)) * slots, :]
         gate = dot(rows_in, whole(j, 0))
         up = dot(rows_in, whole(j, 1))
         hidden = (gate / (1.0 + jnp.exp(-gate)) * up * w).astype(BF)
@@ -306,76 +328,87 @@
             cols = slice(n * 512, (n + 1) * 512)
             part[pair, :, :, :, cols] = dot(p, ys[pair, :, cols], TN).astype(BF).reshape(2, 2, 64, 512)
 
-    near, far = (0, 3), (1, 2)
-    do_x(0)
+    near, middle, last = (1, 2), (3,), (0,)
+    do_x(2)
     forward(7, 1, 0)
-    forward(7, 1, 1)
     for cp in mt:
         cp.wait_recv()
-    gather(0, 0, 0)
-    do_x(1)
-    do_y(3, 0), do_y(1, 0)
-    forward(6, 2, 0)
-    forward(6, 2, 1)
-    gather(0, 1, 3)
-    ready(0)
-    do_x(2)
+    forward(7, 1, 1)
+    gather(0, 0, 1)
+    do_x(3)
     for m in range(3):
         xc[m] = x_send(m, common, COMMON_U)
+    forward(6, 2, 0)
+    for i in (0, 1):
+        do_y(3, i), do_y(1, i), do_y(2, i)
+    do_f(2)
+    forward(6, 2, 1)
+    gather(0, 1, 2)
+    ready(0)
+    do_f(3)
+    expert(0, 0, 0, near)
     forward(5, 3, 0)
-    do_y(3, 1), do_y(1, 1)
-    expert(0, 0, near)
-    do_f(0)
+    do_y(3, 2), do_y(1, 2)
+    do_c(0), do_c(1)
     forward(5, 3, 1)
-    gather(1, 0, 1)
-    do_f(1)
-    do_y(3, 2), do_y(1, 2)
-    do_f(2)
-    ag_r[(4, 0)].wait_recv()
-    ag_l[(4, 1)].wait_recv()
-    gather(1, 1, 2)
-    do_c(0), do_c(1), do_c(2)
-    do_y(2, 0)
-    expert(0, 1, far)
-    do_y(2, 1)
-    for j in (3, 1):
-        ready(j)
-        expert(j, 1, far)
-        if j == 3:
-            do_fc(0), do_fc(1)
+    do_c(2)
+    gather(1, 0, 3)
+    do_y(3, 3), do_y(1, 3)
+    expert(0, 1, 0, middle)
+    ready(3)
+    expert(3, 1, 0, middle)
     do_y(2, 2)
+    do_fc(0), do_fc(1)
+    expert(3, 0, 0, near)
+    ready(1)
+    expert(1, 1, 0, middle)
     do_fc(2)
-    expert(3, 0, near)
+    do_y(2, 3)
+    expert(1, 0, 0, near)
     ready(2)
-    expert(2, 1, far)
+    expert(2, 1, 0, middle)
+    combine(3)
 
     def fold(buf, i, o, b):
         def step(r, carry):
             here = pl.ds(pl.multiple_of(r * 16, 16), 16)
-            buf[i, here, :] = (buf[i, here, :].astype(F32) + part[o // 2, o % 2, b, here, :].astype(F32)).astype(BF)
+            buf[i, here, :] = (buf[i, here, :].astype(F32) + part[ORDER.index(o) // 2, ORDER.index(o) % 2, b, here, :].astype(F32)).astype(BF)
             return carry
         lax.fori_loop(0, 4, step, 0)
 
+    order = ((3, 1), (4, 0), (2, 1), (3, 0), (1, 1), (2, 0), (1, 0))
+    r_in, l_in = {}, {}
+
+    def begin(i):
+        o, b = order[i]
+        r_in[i] = push(half(part, o, b), rr.at[i], at_z(1), head)
+        l_in[i] = push(half(part, 8 - o, 1 - b), ll.at[i], at_z(7), head)
+
+    def onward(i):
+        o, b = order[i]
+        came = order.index((o + 1, b))
+        r_in[came].wait_recv()
+        fold(rr, came, o, b)
+        r_in[i] = push(rr.at[came], rr.at[i], at_z(1), head)
+        l_in[came].wait_recv()
+        fold(ll, came, 8 - o, 1 - b)
+        l_in[i] = push(ll.at[came], ll.at[i], at_z(7), head)
+
+    begin(0)
+    ag_r[(4, 0)].wait_recv()
+    ag_l[(4, 1)].wait_recv()
+    gather(1, 1, 0)
+    for j in range(NX):
+        expert(j, 1, 1, last)
+    combine(0)
+    begin(1)
+    expert(2, 0, 0, near)
     combine(2)
-    r_in, l_in = {}, {}
-    r_in[0] = push(half(part, 4, 0), rr.at[0], at_z(1), head)
-    l_in[0] = push(half(part, 4, 1), ll.at[0], at_z(7), head)
-    l_in[2] = push(half(part, 5, 0), ll.at[2], at_z(7), head)
+    onward(2)
     combine(1)
-    r_in[2] = push(half(part, 3, 1), rr.at[2], at_z(1), head)
-    for j in (1, 2):
-        expert(j, 0, near)
-    combine(3)
-    combine(0)
-    for i, to, step in ((0, 1, 1), (1, 3, 2), (2, 4, 2), (3, 5, 3), (4, 6, 3)):
-        b = {0: 0, 1: 0, 2: 1, 3: 0, 4: 1}[i]
-        r_in[i].wait_recv()
-        fold(rr, i, 4 - step, b)
-        r_in[to] = push(rr.at[i], rr.at[to], at_z(1), head)
-        l_in[i].wait_recv()
-        fold(ll, i, 4 + step, 1 - b)
-        l_in[to] = push(ll.at[i], ll.at[to], at_z(7), head)
-    for b, (ri, li) in enumerate(((5, 6), (6, 5))):
+    for i in range(3, 7):
+        onward(i)
+    for b, (ri, li) in enumerate(((6, 4), (4, 6))):
         r_in[ri].wait_recv()
         l_in[li].wait_recv()
 
@@ -404,7 +437,7 @@
         out_specs=vmem,
         scratch_shapes=[
             V((tok_dev, width), BF), V((tok_dev, width), BF), V((tok_dev, width), BF),
-            V((tok_dev, width), F32), V((NY * NC, block_rows, width), BF), V((NY * NC - 1, block_rows, width), BF),
+            V((tok_dev, width), F32), V((2, NY * NC, block_rows // 2, width), BF), V((2, NY * NC - 1, block_rows // 2, width), BF),
             V((NZ // 2, 2, 2, block_rows // 2, dim), BF),
             V((NX, 3, UNITS, dim // UNITS, hidden), BF),
             V((2, NX, 4 * CAP, dim), BF), V((NZ // 2, NX * 2 * CAP, dim), BF),

time: 138 us -> 135 us (0.978)
  Pallas kernels: 136 us -> 133 us
    pallas_call x1, Pallas kernels: 136 us -> 133 us  [body(): pl.pallas_call(kernel, out_shape=jax.ShapeDtypeStruct((block_rows, dim),...]
where the time goes in v4:
time: 135 us; the launch traced here: 134 us
  Pallas kernels  133 us (99%)
  local copies, waits for them, and re-layouts  1.88 us (1%)
    pallas_call x1, Pallas kernels, body(): pl.pallas_call(kernel, out_shape=jax.ShapeDtypeStruct((block_rows, dim),...  133 us

profile of v4, /device:TPU:1, one launch (start us, length us, event | category | flops | bytes accessed | tf_op | source)
XLA Modules:
  0.0 134.4 jit_solution(8189959724677802251)
XLA Ops:
  0.0 132.5 %shard_map.82 = bf16[128,2048]{1,0:T(8,128)(2,1)} custom-call(bf16[1024,256]{1,0:T(8,128)(2,1)} %q_hbm.1, bf16[1024,256]{1,0:T(8,128)(2,1)} %k_hbm.1, bf16[1024,256]{1,0:T(8,128)(2,1)} %v_hbm.1, bf16[32,2048]{1,0:T(8,128)(2,1)} %bitcast.8, bf16[32,64,512]{2,1,0:T(8,128)(2,1)} %bitcast.5, bf16[32,64,512]{2,1,0:T(8,128)(2,1)} %bitcast.6, ...), custom_call_target="tpu_custom_call" | custom-call | flops 10000000000 | bytes 10000000 | tf_op jit(solution)/shard_map/pallas_call | solution.py:433
  132.5 1.9 %copy.10 = bf16[128,2048]{1,0:T(8,128)(2,1)} copy(bf16[128,2048]{1,0:T(8,128)(2,1)} %shard_map.82) | data formatting | bytes 1048576

commit v5 on v4

--- a/solution.py
+++ b/solution.py
@@ -14,11 +14,11 @@
 BF, F32 = jnp.bfloat16, jnp.float32
 MESH = pl.DeviceIdType.MESH
 NN, NT, TN = (((1,), (0,)), ((), ())), (((1,), (1,)), ((), ())), (((0,), (0,)), ((), ()))
-FLOWS = 160
+FLOWS = 192
 UNITS, COMMON_U = 32, 2
 OWN_U = (UNITS - 2 * COMMON_U) // 4
 ORDER = (0, 4, 1, 7, 2, 6, 3, 5)
-PIECES = ((0, 0, 3), (0, 3, OWN_U - 3), (1, 0, OWN_U), (2, 0, OWN_U))
+PIECES = ((0, 0, 3), (0, 3, OWN_U - 3), (1, 0, OWN_U), (2, 0, 4), (2, 4, OWN_U - 4))
 
 
 def dot(a, b, dims=NN):
@@ -215,6 +215,7 @@
         cp.wait_recv()
     send(2)
     send(3)
+    send(4)
     carried = cz[...].reshape(2 * HD, HD)
     high = carried.astype(BF)
     car[0] = high
@@ -333,11 +334,12 @@
     forward(7, 1, 0)
     for cp in mt:
         cp.wait_recv()
+    do_x(3)
     forward(7, 1, 1)
-    gather(0, 0, 1)
-    do_x(3)
+    do_x(4)
     for m in range(3):
         xc[m] = x_send(m, common, COMMON_U)
+    gather(0, 0, 1)
     forward(6, 2, 0)
     for i in (0, 1):
         do_y(3, i), do_y(1, i), do_y(2, i)
@@ -346,6 +348,7 @@
     gather(0, 1, 2)
     ready(0)
     do_f(3)
+    do_f(4)
     expert(0, 0, 0, near)
     forward(5, 3, 0)
     do_y(3, 2), do_y(1, 2)
@@ -353,7 +356,8 @@
     forward(5, 3, 1)
     do_c(2)
     gather(1, 0, 3)
-    do_y(3, 3), do_y(1, 3)
+    for i in (3, 4):
+        do_y(3, i), do_y(1, i)
     expert(0, 1, 0, middle)
     ready(3)
     expert(3, 1, 0, middle)
@@ -363,7 +367,7 @@
     ready(1)
     expert(1, 1, 0, middle)
     do_fc(2)
-    do_y(2, 3)
+    do_y(2, 3), do_y(2, 4)
     expert(1, 0, 0, near)
     ready(2)
     expert(2, 1, 0, middle)

time: 135 us -> 136 us (level)
  no operation moved by 1% of the time
where the time goes in v5:
time: 136 us; the launch traced here: 135 us
  Pallas kernels  134 us (99%)
  local copies, waits for them, and re-layouts  1.88 us (1%)
    pallas_call x1, Pallas kernels, body(): pl.pallas_call(kernel, out_shape=jax.ShapeDtypeStruct((block_rows, dim),...  134 us

profile of v5, /device:TPU:1, one launch (start us, length us, event | category | flops | bytes accessed | tf_op | source)
XLA Modules:
  0.0 135.4 jit_solution(3021055545554085324)
XLA Ops:
  0.0 133.5 %shard_map.82 = bf16[128,2048]{1,0:T(8,128)(2,1)} custom-call(bf16[1024,256]{1,0:T(8,128)(2,1)} %q_hbm.1, bf16[1024,256]{1,0:T(8,128)(2,1)} %k_hbm.1, bf16[1024,256]{1,0:T(8,128)(2,1)} %v_hbm.1, bf16[32,2048]{1,0:T(8,128)(2,1)} %bitcast.8, bf16[32,64,512]{2,1,0:T(8,128)(2,1)} %bitcast.5, bf16[32,64,512]{2,1,0:T(8,128)(2,1)} %bitcast.6, ...), custom_call_target="tpu_custom_call" | custom-call | flops 10000000000 | bytes 10000000 | tf_op jit(solution)/shard_map/pallas_call | solution.py:437
  133.5 1.9 %copy.10 = bf16[128,2048]{1,0:T(8,128)(2,1)} copy(bf16[128,2048]{1,0:T(8,128)(2,1)} %shard_map.82) | data formatting | bytes 1048576
